TPU v7x, 128 devices: a whole 4x4x4 slice. The times are simulated.
128 devices in a mesh: island: 4 (over x_lo, core), fsdp: 16 (over y, z), tp: 2 (over x_hi).
Axes of the slice: x: 4 (x_hi: 2, x_lo: 2; x = x_hi * 2 + x_lo), y: 4, z: 4, core: 2. Of those that a mesh axis runs over, the one named last changes fastest.
Arguments:
- local_weights: bfloat16 [4, 4, 1024, 12288], P('island', None, 'fsdp', 'tp'), may hold values from -6 to 6
- outer_base: bfloat16 [3, 1024, 12288], P(None, 'fsdp', 'tp'), may hold values from -6 to 6
- momentum: float32 [3, 1024, 12288], P(None, 'fsdp', 'tp'), may hold values from -6 to 6
- layer_order: int32 [4], replicated, may hold values from 0 to 3, each once
- features: bfloat16 [4, 8192, 12288], P('island', 'fsdp', 'tp'), may hold values from -6 to 6
- targets: bfloat16 [4, 8192, 1024], P('island', 'fsdp'), may hold values from -6 to 6
Outputs:
- new_base: bfloat16 [3, 1024, 12288], P(None, 'fsdp', 'tp')
- new_momentum: float32 [3, 1024, 12288], P(None, 'fsdp', 'tp')
- inner_grad: float32 [4, 1024, 12288], P('island', 'fsdp', 'tp')
Inputs may be any that keep to these rules, and one draw needn't show every extreme that they name: `layer_order`: a permutation of the window's layers.
All inputs are finite; a program needn't handle non-finite values. Where the computation divides by a largest or mean magnitude, that divisor is 1e-20 or more.
Results may differ from a plain program's by a relative error of at most 0.024.
Values may be sent and summed in bfloat16 or wider, within the bound.
A program may use at most 128 MiB of HBM per device.

v0:
```python
import jax
import jax.numpy as jnp
from jax import lax
from jax.sharding import PartitionSpec as P

D = 12288
FRAG = 3
QB = 32


outer_mu = 0.9
outer_rate = 0.7
scale_eps = 1e-06


def per_device(local_weights, outer_base, momentum, layer_order, features, targets):
    key_scale = D ** (-0.5)
    own_layers = local_weights[0]
    tokens_in = features[0]
    target_keys = targets[0]
    inner_w = lax.dynamic_index_in_dim(own_layers, layer_order[FRAG], 0, keepdims=False)
    partial_keys = lax.dot_general(
        tokens_in,
        lax.all_gather(inner_w, "fsdp", axis=0, tiled=True),
        (((1,), (1,)), ((), ())),
        preferred_element_type=jnp.float32,
    )
    keys = lax.psum(partial_keys.astype(jnp.bfloat16), "tp").astype(jnp.float32) * key_scale
    residual = (keys - target_keys.astype(jnp.float32)).astype(jnp.bfloat16)
    own_grad = lax.psum_scatter(
        (
            lax.dot_general(
                residual, tokens_in, (((0,), (0,)), ((), ())), preferred_element_type=jnp.float32
            )
            * key_scale
        ).astype(jnp.bfloat16),
        "fsdp",
        scatter_dimension=0,
        tiled=True,
    ).astype(jnp.float32)
    frag_layers = jnp.take(own_layers, layer_order[:FRAG], axis=0)
    base_f32 = outer_base.astype(jnp.float32)
    drift = frag_layers.astype(jnp.float32) - base_f32
    frag_n, rows_n, cols_n = drift.shape
    blocks = drift.reshape(frag_n, rows_n, cols_n // QB, QB)
    block_scale = (jnp.max(jnp.abs(blocks), axis=-1) + scale_eps).astype(jnp.bfloat16)
    quantized = (blocks / block_scale.astype(jnp.float32)[..., None]).astype(jnp.bfloat16)
    quantized = lax.optimization_barrier(quantized)
    restored = quantized.astype(jnp.float32) * block_scale.astype(jnp.float32)[..., None]
    summed = lax.psum(restored.astype(jnp.bfloat16), "island").astype(jnp.float32)
    mean_drift = summed.reshape(frag_n, rows_n, cols_n) / lax.axis_size("island")
    moment_new = outer_mu * momentum + mean_drift
    base_new = (base_f32 + outer_rate * (mean_drift + outer_mu * moment_new)).astype(jnp.bfloat16)
    return (base_new, moment_new, own_grad[None])


def solution(mesh):
    return jax.shard_map(
        per_device,
        mesh=mesh,
        in_specs=(
            P("island", None, "fsdp", "tp"),
            P(None, "fsdp", "tp"),
            P(None, "fsdp", "tp"),
            P(),
            P("island", "fsdp", "tp"),
            P("island", "fsdp", None),
        ),
        out_specs=(P(None, "fsdp", "tp"), P(None, "fsdp", "tp"), P("island", "fsdp", "tp")),
        check_vma=False,
    )
```

profile of v0, /device:TPU:8, one launch (start us, length us, event | category | flops | bytes accessed | tf_op | source)
XLA Modules:
  0.0 374.7 jit_solution(14094840725499965790)
XLA Ops:
  7.2 0.0 copy-start
  7.2 0.0 all-gather.3.cloned.1.call-start
  7.2 1.4 slice.7
  10.6 0.0 copy-done
  10.6 0.9 constant_dynamic-slice_fusion
  11.5 0.0 all-gather.3.cloned.1.call-update
  11.5 0.0 all-reduce.5.cloned.1.call-start
  11.6 0.7 compare_and_fusion
  12.3 2.2 gather_fusion
  14.4 5.4 %convert_subtract_fusion = f32[3,64,6144]{2,1,0:T(8,128)} fusion(bf16[3,64,6144]{2,1,0:T(8,128)(2,1)} %param.7, bf16[3,64,6144]{2,1,0:T(8,128)(2,1)} %gather_fusion, pred[3]{0:T(512)(128)(4,1)S(1)} %get-tuple-element.5), kind=kLoop, calls=%fused_computation.11 | loop fusion | flops 4718592 | bytes 9437187 | tf_op jit(solution)/shard_map/sub | solution.py:43
  19.8 7.9 %copy.9 = f32[3,64,6144]{1,2,0:T(8,128)} copy(f32[3,64,6144]{2,1,0:T(8,128)} %convert_subtract_fusion) | data formatting | bytes 9437184 | tf_op jit(solution)/shard_map/sub | solution.py:43
  27.8 6.1 %abs_reduce_fusion = f32[3,64,192]{1,2,0:T(8,128)S(1)} fusion(f32[3,64,192,32]{1,3,2,0:T(8,128)} %bitcast.32), kind=kLoop, calls=%fused_computation.7 | loop fusion | flops 2322432 | bytes 4866048 | tf_op jit(solution)/shard_map/reduce_max | solution.py:46
  34.0 70.1 %all-gather.3.cloned.1.call-done = bf16[1,1,1024,6144]{3,2,1,0:T(8,128)(2,1)} async-done(((bf16[1,1,64,6144]{3,2,1,0:T(8,128)(2,1)}), bf16[1,1,1024,6144]{3,2,1,0:T(8,128)(2,1)}) %all-gather.3.cloned.1.call-update) | async-done | bytes 12582928 | tf_op jit(solution)/shard_map/all_gather | solution.py:24
  104.1 12.3 %fusion.11 = bf16[512,1024]{1,0:T(8,128)(2,1)} fusion(bf16[1,512,6144]{2,1,0:T(8,128)(2,1)} %param.10, bf16[1,1,1024,6144]{3,2,1,0:T(8,128)(2,1)} %all-gather.3.cloned.1.call-done), kind=kOutput, calls=%fused_computation.17 | convolution fusion | flops 6442975232 | bytes 19922944 | tf_op jit(solution)/shard_map/dot_general | solution.py:22
  116.4 0.0 all-reduce.5.cloned.1.call-update
  116.4 0.0 all-reduce.3.cloned.1.call-start
  116.4 5.1 %divide_convert_fusion = bf16[3,64,192,32]{1,3,2,0:T(8,128)(2,1)S(1)} fusion(f32[3,64,192,32]{1,3,2,0:T(8,128)} %bitcast.33, f32[3,64,192]{1,2,0:T(8,128)S(1)} %fusion.19), kind=kLoop, calls=%fused_computation.6 | loop fusion | flops 2359296 | bytes 7225344 | tf_op jit(solution)/shard_map/convert_element_type | solution.py:47
  121.6 3.3 multiply_convert_fusion.1
  124.9 0.0 copy-start.2
  124.9 0.0 all-reduce.3.cloned.1.call-update
  124.9 0.2 reduce-scatter.2.cloned.1.call-start
  125.2 39.1 %all-reduce.5.cloned.1.call-done = bf16[512,1024]{1,0:T(8,128)(2,1)} async-done(((bf16[512,1024]{1,0:T(8,128)(2,1)}), bf16[512,1024]{1,0:T(8,128)(2,1)}) %all-reduce.5.cloned.1.call-update) | async-done | bytes 1048592 | tf_op jit(solution)/shard_map/psum | solution.py:28
  164.3 0.0 copy-done.2
  164.3 12.1 %multiply_convert_fusion = bf16[1024,6144]{1,0:T(8,128)(2,1)} fusion(bf16[1,512,6144]{2,1,0:T(8,128)(2,1)} %param.10, bf16[512,1024]{1,0:T(8,128)(2,1)} %all-reduce.5.cloned.1.call-done, bf16[1,512,1024]{2,1,0:T(8,128)(2,1)S(1)} %copy-done.2), kind=kOutput, calls=%fused_computation.1 | convolution fusion | flops 6457655296 | bytes 20971520 | tf_op jit(solution)/shard_map/dot_general | solution.py:32
  176.4 0.0 reduce-scatter.2.cloned.1.call-update
  176.4 90.5 %all-reduce.3.cloned.1.call-done = bf16[3,64,192,32]{1,3,2,0:T(8,128)(2,1)} async-done(((bf16[3,64,192,32]{1,3,2,0:T(8,128)(2,1)}), bf16[3,64,192,32]{1,3,2,0:T(8,128)(2,1)}) %all-reduce.3.cloned.1.call-update) | async-done | bytes 2359312 | tf_op jit(solution)/shard_map/psum | solution.py:50
  266.9 7.4 %convert_multiply_fusion = f32[3,64,192,32]{1,3,2,0:T(8,128)} fusion(bf16[3,64,192,32]{1,3,2,0:T(8,128)(2,1)} %all-reduce.3.cloned.1.call-done), kind=kLoop, calls=%fused_computation.4 | loop fusion | flops 2359296 | bytes 7077888 | tf_op jit(solution)/shard_map/div | solution.py:51
  274.3 8.6 %copy.11 = f32[3,64,6144]{2,1,0:T(8,128)} copy(f32[3,64,6144]{1,2,0:T(8,128)} %bitcast.34) | data formatting | bytes 9437184 | tf_op jit(solution)/shard_map/div | solution.py:51
  282.9 9.1 %fusion.4 = (bf16[3,64,6144]{2,1,0:T(8,128)(2,1)}, f32[3,64,6144]{2,1,0:T(8,128)}) fusion(bf16[3,64,6144]{2,1,0:T(8,128)(2,1)} %param.7, f32[3,64,6144]{2,1,0:T(8,128)} %copy.11, f32[3,64,6144]{2,1,0:T(8,128)} %param.8), kind=kLoop, calls=%fused_computation.12 | loop fusion | flops 9437184 | bytes 18874368 | tf_op jit(solution)/shard_map/convert_element_type | solution.py:53
  292.0 73.8 %reduce-scatter.2.cloned.1.call-done = bf16[64,6144]{1,0:T(8,128)(2,1)} async-done(((bf16[1024,6144]{1,0:T(8,128)(2,1)}), bf16[64,6144]{1,0:T(8,128)(2,1)}) %reduce-scatter.2.cloned.1.call-update) | async-done | bytes 786448 | tf_op jit(solution)/shard_map/reduce_scatter | solution.py:30
  365.8 2.4 bitcast_convert_fusion
  368.2 0.0 copy-done.1
  (3 shorter events, 0.0 us)
Async XLA Ops:
  7.2 3.4 copy-start
  7.2 96.9 %all-gather.3.cloned.1.call-start = ((), (), s32[]{:S(2)}) async-start(), calls=%async_computation.4 | async-start | bytes 13369344 | tf_op jit(solution)/shard_map/all_gather | solution.py:24
  11.5 152.8 %all-reduce.5.cloned.1.call-start = ((), (), s32[]{:S(2)}) async-start(), calls=%async_computation.2 | async-start | bytes 2097152 | tf_op jit(solution)/shard_map/psum | solution.py:28
  116.4 150.5 %all-reduce.3.cloned.1.call-start = ((), (), s32[]{:S(2)}) async-start(), calls=%async_computation.1 | async-start | bytes 9437184 | tf_op jit(solution)/shard_map/psum | solution.py:50
  124.9 39.4 %copy-start.2 = (bf16[1,512,1024]{2,1,0:T(8,128)(2,1)S(1)}, bf16[1,512,1024]{2,1,0:T(8,128)(2,1)}, u32[]{:S(2)}) copy-start(bf16[1,512,1024]{2,1,0:T(8,128)(2,1)} %param.11) | copy-start | bytes 3145732
  124.9 240.9 %reduce-scatter.2.cloned.1.call-start = ((), (), s32[]{:S(2)}) async-start(), calls=%async_computation.3 | async-start | bytes 13369344 | tf_op jit(solution)/shard_map/reduce_scatter | solution.py:30
  282.9 85.3 %copy-start.1 = (bf16[1,4,64,6144]{3,2,1,0:T(8,128)(2,1)S(1)}, bf16[1,4,64,6144]{3,2,1,0:T(8,128)(2,1)}, u32[]{:S(2)}) copy-start(bf16[1,4,64,6144]{3,2,1,0:T(8,128)(2,1)} %param.6) | copy-start | bytes 9437188
Sparse Core Ops, SparseCore 0:
  11.7 92.3 all-gather.2
  116.5 47.7 all-reduce.4
  167.5 99.3 all-reduce.2
  270.6 95.1 reduce-scatter.1
where the time goes:
time: 377 us; the launch traced here: 375 us
  waiting for transfers between devices  274 us (73%)
  other arithmetic  39.6 us (11%)
  matrix products  24.4 us (6%)
  local copies, waits for them, and re-layouts  21 us (6%)
  between operations  15.7 us (4%)
    psum x1, waiting for transfers between devices, per_device(): lax.psum(restored.astype(jnp.bfloat16), 'island').astype(jnp.float32)  90.5 us
    reduce_scatter x1, waiting for transfers between devices, per_device(): lax.psum_scatter((lax.dot_general(residual, tokens_in, (((0,), (0,)), (()...  73.8 us
    all_gather x1, waiting for transfers between devices, per_device(): lax.all_gather(inner_w, 'fsdp', axis=0, tiled=True)  70.1 us
    psum x1, waiting for transfers between devices, per_device(): lax.psum(partial_keys.astype(jnp.bfloat16), 'tp').astype(jnp.float32)  39.1 us
    dot_general x1, matrix products, per_device(): lax.dot_general(tokens_in, lax.all_gather(inner_w, 'fsdp', axis=0, tiled=...  12.3 us
    dot_general x1, matrix products, per_device(): lax.dot_general(residual, tokens_in, (((0,), (0,)), ((), ())), preferred_...  12.1 us
    convert_element_type x1, other arithmetic, per_device(): (base_f32 + outer_rate * (mean_drift + outer_mu * moment_new)).astype(jnp...  9.15 us
    div x1, local copies, waits for them, and re-layouts, per_device(): summed.reshape(frag_n, rows_n, cols_n) / lax.axis_size('island')  8.58 us
  transfers between devices with their start and end apart: 4, of which 4 were waited for; matrix products, arithmetic and copies ran while one was open for 18% of the time, Pallas kernels for 0%

commit v1 on v0

v1 whole, which is shorter than its diff:
```python
import jax
import jax.numpy as jnp
from jax import lax
from jax.experimental import pallas as pl
from jax.experimental.pallas import tpu as pltpu
from jax.sharding import PartitionSpec as P

D = 12288
FRAG = 3
QB = 32
KEY_SCALE = D ** (-0.5)

outer_mu = 0.9
outer_rate = 0.7
scale_eps = 1e-06

MESH = pl.DeviceIdType.MESH
BF = jnp.bfloat16
F32 = jnp.float32

HALF = 3072
TT = 256
NT = 2
NCH = 4
QC = 1536
NQ = HALF // QC
NU = NCH * NQ
QT = 512


def nt_dot(a, b):
    return lax.dot_general(a, b, (((1,), (1,)), ((), ())), preferred_element_type=F32)


def kernel(
    lo_ref, lw_hbm, base_hbm, x_hbm, t_hbm,
    og_ref, os_ref,
    lw, base, tt, tpm, xv, wv, wp, ka, kb, kr, ts, tr, rv, gv, r1, r2, sv, nr, uv, pr,
    qo, qs, qr, s2, xr, tot, fr,
    loc_sem, wz_s, wz_r, wp_s, wp_r, wn_s, wn_r, x_s, x_r, kb_s, kb_r, tp_s, tp_r, rr_s, rr_r,
    g_s, g_r, nb_s, nb_r, pr_s, pr_r, q_s, q_r, xl_s, xl_r, fr_s, fr_r,
):
    isl = lax.axis_index("island")
    f = lax.axis_index("fsdp")
    tpi = lax.axis_index("tp")
    core = lax.rem(isl, 2)
    y = lax.div(f, 4)
    z = lax.rem(f, 4)
    yy = lax.rem(y + 3 * core, 4)
    pp = yy + 1 - 2 * lax.rem(yy, 2)
    h = lax.rem(lax.div(yy + 1, 2), 2)
    yp = lax.rem(pp + core, 4)
    yn = lax.rem(3 - yy + core, 4)
    ynp = lax.rem(3 - pp + core, 4)
    yo = [y, yp, yn, ynp]
    zr = lax.rem(z + 1, 4)
    zl = lax.rem(z + 3, 4)
    z2 = lax.rem(z + 2, 4)
    d_pair = {"fsdp": yp * 4 + z}
    d_nb = {"fsdp": yn * 4 + z}
    d_right = {"fsdp": y * 4 + zr}
    d_left = {"fsdp": y * 4 + zl}
    d_tp = {"tp": 1 - tpi}
    d_core = {"island": isl + 1 - 2 * core}
    d_xlo = {"island": lax.rem(isl + 2, 4)}

    mine = pl.ds(pl.multiple_of(h * HALF, HALF), HALF)
    other = pl.ds(pl.multiple_of((1 - h) * HALF, HALF), HALF)

    cp_lw = pltpu.make_async_copy(lw_hbm, lw, loc_sem.at[0])
    cp_lw.start()
    cp_base = pltpu.make_async_copy(base_hbm, base, loc_sem.at[1])
    cp_base.start()
    cp_x = pltpu.make_async_copy(x_hbm.at[:, mine], xv.at[0], loc_sem.at[2])
    cp_x.start()
    cp_t = pltpu.make_async_copy(t_hbm, tt, loc_sem.at[3])
    cp_t.start()

    barrier = pltpu.get_barrier_semaphore()
    for dev in (d_pair, d_nb, d_right, d_left, d_tp, d_core, d_xlo):
        pl.semaphore_signal(barrier, inc=1, device_id=dev, device_id_type=MESH)
    pl.semaphore_wait(barrier, 7)

    started = []

    def copy(src, dst, ss, rs, dev):
        return pltpu.make_async_remote_copy(
            src_ref=src, dst_ref=dst, send_sem=ss, recv_sem=rs, device_id=dev, device_id_type=MESH
        )

    def send(src, dst, ss, rs, dev):
        c = copy(src, dst, ss, rs, dev)
        c.start()
        started.append(c)

    def wait_recv(dst, ss, rs, dev):
        copy(dst, dst, ss, rs, dev).wait_recv()

    def wslot(zo, p, lo, n):
        return wv.at[zo * 4 + yo[p], pl.ds(lo, n)]

    def w_zsend(p, r):
        piece = wslot(z, p, r * 32, 32)
        send(piece, piece, wz_s.at[r, p, 0], wz_r.at[r, p, 0], d_right)
        send(piece, piece, wz_s.at[r, p, 1], wz_r.at[r, p, 1], d_left)

    def w_fwd(p, r):
        wait_recv(wslot(zl, p, r * 32, 32), wz_s.at[r, p, 0], wz_r.at[r, p, 0], d_right)
        a = wslot(zl, p, r * 32, 16)
        send(a, a, wz_s.at[r, p, 2], wz_r.at[r, p, 2], d_right)
        wait_recv(wslot(zr, p, r * 32, 32), wz_s.at[r, p, 1], wz_r.at[r, p, 1], d_left)
        b = wslot(zr, p, r * 32 + 16, 16)
        send(b, b, wz_s.at[r, p, 3], wz_r.at[r, p, 3], d_left)

    def w_end(p, r):
        wait_recv(wslot(z2, p, r * 32, 16), wz_s.at[r, p, 2], wz_r.at[r, p, 2], d_right)
        wait_recv(wslot(z2, p, r * 32 + 16, 16), wz_s.at[r, p, 3], wz_r.at[r, p, 3], d_left)

    def w_pair_send(r):
        send(wp.at[pl.ds(r * 32, 32)], wslot(z, 0, r * 32, 32), wp_s.at[r], wp_r.at[r], d_pair)

    def w_nb_send(p, r):
        piece = wslot(z, p, r * 32, 32)
        send(piece, piece, wn_s.at[p, r], wn_r.at[p, r], d_nb)

    def w_pair_got(r):
        wait_recv(wslot(z, 1, r * 32, 32), wp_s.at[r], wp_r.at[r], d_pair)

    def w_nb_got(p, r):
        wait_recv(wslot(z, 2 + p, r * 32, 32), wn_s.at[p, r], wn_r.at[p, r], d_nb)

    def x_send(t):
        rows = pl.ds(t * TT, TT)
        send(x_hbm.at[rows, other], xv.at[1, rows], x_s.at[t], x_r.at[t], d_pair)

    def x_got(t):
        wait_recv(xv.at[1, pl.ds(t * TT, TT)], x_s.at[t], x_r.at[t], d_pair)

    def chunk_w(c):
        return wv[:, pl.ds(c * 16, 16), :].reshape(256, HALF)

    def key_own(c):
        for t in range(NT):
            ka[c, t] = nt_dot(chunk_w(c), xv[0, pl.ds(t * TT, TT), :])

    def key_pair(c, t):
        kb[c, t] = nt_dot(chunk_w(c), xv[1, pl.ds(t * TT, TT), :]).astype(BF)
        send(kb.at[c, t], kr.at[c, t], kb_s.at[c, t], kb_r.at[c, t], d_pair)

    def key_mid(c, t):
        wait_recv(kr.at[c, t], kb_s.at[c, t], kb_r.at[c, t], d_pair)
        k = ka[c, t] + kr[c, t].astype(F32)
        ka[c, t] = k
        ts[c, t] = k.astype(BF)
        send(ts.at[c, t], tr.at[c, t], tp_s.at[c, t], tp_r.at[c, t], d_tp)

    def key_res(c, t):
        wait_recv(tr.at[c, t], tp_s.at[c, t], tp_r.at[c, t], d_tp)
        keys = (ka[c, t] + tr[c, t].astype(F32)) * KEY_SCALE
        rv[0, c, t] = (keys - tpm[c, :, t * TT:(t + 1) * TT].astype(F32)).astype(BF)
        send(rv.at[0, c, t], rv.at[1, c, t], rr_s.at[c, t], rr_r.at[c, t], d_pair)

    def key_done(c):
        for t in range(NT):
            wait_recv(rv.at[1, c, t], rr_s.at[c, t], rr_r.at[c, t], d_pair)

    def targets_chunk(c):
        row = lax.broadcasted_iota(jnp.int32, (256, 1024), 0)
        col = lax.broadcasted_iota(jnp.int32, (256, 1024), 1)
        slot = row >> 4
        want = ((slot & 3) * 4 + (slot >> 2)) * 64 + c * 16 + (row & 15)
        pick = jnp.where(col == want, 1.0, 0.0).astype(BF)
        tpm[c] = nt_dot(pick, tt[...]).astype(BF)

    def gpart(zo, lo, n, c, q):
        return gv.at[pl.ds(zo * 4 + lo, n), pl.ds(c * 16, 16), pl.ds(q * QC, QC)]

    def grad_unit(u):
        c, q = u // NQ, u % NQ

        @pl.loop(0, QC // 512)
        def _(n):
            cols = pl.ds(pl.multiple_of(q * QC + n * 512, 512), 512)
            acc = None
            for i in range(2):
                for t in range(NT):
                    part = jnp.dot(
                        rv[i, c, t], xv[i, pl.ds(t * TT, TT), cols], preferred_element_type=F32
                    )
                    acc = part if acc is None else acc + part
            gv[:, pl.ds(c * 16, 16), cols] = (acc * KEY_SCALE).astype(BF).reshape(16, 16, 512)

        send(gpart(z2, 0, 2, c, q), r1.at[0, u], g_s.at[u, 0], g_r.at[u, 0], d_right)
        send(gpart(z2, 2, 2, c, q), r1.at[1, u], g_s.at[u, 1], g_r.at[u, 1], d_left)
        send(gpart(zr, 2, 2, c, q), r2.at[0, u, pl.ds(2, 2)], g_s.at[u, 2], g_r.at[u, 2], d_right)
        send(gpart(zl, 0, 2, c, q), r2.at[1, u, pl.ds(0, 2)], g_s.at[u, 3], g_r.at[u, 3], d_left)

    def grad_fwd(u):
        c, q = u // NQ, u % NQ
        rows, cols = pl.ds(c * 16, 16), pl.ds(q * QC, QC)
        wait_recv(r1.at[0, u], g_s.at[u, 0], g_r.at[u, 0], d_right)
        sl = pl.ds(zr * 4, 2)
        gv[sl, rows, cols] = (gv[sl, rows, cols].astype(F32) + r1[0, u].astype(F32)).astype(BF)
        send(gpart(zr, 0, 2, c, q), r2.at[0, u, pl.ds(0, 2)], g_s.at[u, 4], g_r.at[u, 4], d_right)
        wait_recv(r1.at[1, u], g_s.at[u, 1], g_r.at[u, 1], d_left)
        sl2 = pl.ds(zl * 4 + 2, 2)
        gv[sl2, rows, cols] = (gv[sl2, rows, cols].astype(F32) + r1[1, u].astype(F32)).astype(BF)
        send(gpart(zl, 2, 2, c, q), r2.at[1, u, pl.ds(2, 2)], g_s.at[u, 5], g_r.at[u, 5], d_left)

    def grad_ring(u):
        c, q = u // NQ, u % NQ
        wait_recv(r2.at[0, u, pl.ds(2, 2)], g_s.at[u, 2], g_r.at[u, 2], d_right)
        wait_recv(r2.at[1, u, pl.ds(0, 2)], g_s.at[u, 3], g_r.at[u, 3], d_left)
        wait_recv(r2.at[0, u, pl.ds(0, 2)], g_s.at[u, 4], g_r.at[u, 4], d_right)
        wait_recv(r2.at[1, u, pl.ds(2, 2)], g_s.at[u, 5], g_r.at[u, 5], d_left)
        own = gv[pl.ds(z * 4, 4), pl.ds(c * 16, 16), pl.ds(q * QC, QC)].astype(F32)
        sv[u] = (own + r2[0, u].astype(F32) + r2[1, u].astype(F32)).astype(BF)
        send(sv.at[u, yn], nr.at[u, 0], nb_s.at[u, 0], nb_r.at[u, 0], d_nb)
        send(sv.at[u, ynp], nr.at[u, 1], nb_s.at[u, 1], nb_r.at[u, 1], d_nb)

    def grad_pair(u):
        c, q = u // NQ, u % NQ
        wait_recv(nr.at[u, 1], nb_s.at[u, 1], nb_r.at[u, 1], d_nb)
        uv[u] = (sv[u, yp].astype(F32) + nr[u, 1].astype(F32)).astype(BF)
        send(uv.at[u], pr.at[u], pr_s.at[u], pr_r.at[u], d_pair)
        wait_recv(nr.at[u, 0], nb_s.at[u, 0], nb_r.at[u, 0], d_nb)
        cols = pl.ds(pl.multiple_of(h * HALF + q * QC, QC), QC)
        og_ref[c * 16:(c + 1) * 16, cols] = (sv[u, y].astype(F32) + nr[u, 0].astype(F32)).astype(BF)

    def grad_out(u):
        c, q = u // NQ, u % NQ
        wait_recv(pr.at[u], pr_s.at[u], pr_r.at[u], d_pair)
        cols = pl.ds(pl.multiple_of((1 - h) * HALF + q * QC, QC), QC)
        og_ref[c * 16:(c + 1) * 16, cols] = pr[u]

    sel_r = lax.broadcasted_iota(jnp.int32, (128, 128), 0)
    sel_c = lax.broadcasted_iota(jnp.int32, (128, 128), 1)

    def quantize(fi):
        layer = lo_ref[fi]

        def half_of(side, dst):
            @pl.loop(0, HALF // QT)
            def _(j):
                pick = jnp.where(sel_r == (sel_c | (QB - 1)), 1.0, 0.0).astype(BF)
                for k in range(QT // 128):
                    col = pl.multiple_of(side * HALF + j * QT + k * 128, 128)
                    a = lw[layer, :, pl.ds(col, 128)].astype(F32)
                    b = base[fi, :, pl.ds(col, 128)].astype(F32)
                    drift = a - b
                    m = jnp.abs(drift)
                    for s in (1, 2, 4, 8, 16):
                        m = jnp.maximum(m, pltpu.roll(m, s, 1))
                    sc = jnp.dot((m + scale_eps).astype(BF), pick, preferred_element_type=F32)
                    quant = (drift / sc).astype(BF).astype(F32)
                    out = pl.multiple_of(j * QT + k * 128, 128)
                    dst[fi, :, pl.ds(out, 128)] = (quant * sc).astype(BF)

        half_of(1 - core, qs)
        send(qs.at[fi], qr.at[fi], q_s.at[fi], q_r.at[fi], d_core)
        half_of(core, qo)

    def tiles(body):
        @pl.loop(0, HALF // QT)
        def _(j):
            body(pl.ds(pl.multiple_of(j * QT, QT), QT), j)

    def outer_core(fi):
        wait_recv(qr.at[fi], q_s.at[fi], q_r.at[fi], d_core)

        def body(cols, j):
            s2[fi, :, cols] = (qo[fi, :, cols].astype(F32) + qr[fi, :, cols].astype(F32)).astype(BF)

        tiles(body)
        send(s2.at[fi], xr.at[fi], xl_s.at[fi], xl_r.at[fi], d_xlo)

    def outer_x(fi):
        wait_recv(xr.at[fi], xl_s.at[fi], xl_r.at[fi], d_xlo)

        def body(cols, j):
            v = (s2[fi, :, cols].astype(F32) + xr[fi, :, cols].astype(F32)).astype(BF)
            tot[fi, :, cols] = v
            os_ref[fi, :, pl.ds(pl.multiple_of(core * HALF + j * QT, QT), QT)] = v

        tiles(body)
        send(tot.at[fi], fr.at[fi], fr_s.at[fi], fr_r.at[fi], d_core)

    def outer_end(fi):
        wait_recv(fr.at[fi], fr_s.at[fi], fr_r.at[fi], d_core)

        def body(cols, j):
            os_ref[fi, :, pl.ds(pl.multiple_of((1 - core) * HALF + j * QT, QT), QT)] = fr[fi, :, cols]

        tiles(body)

    cp_lw.wait()
    inner = lo_ref[FRAG]
    wv[z * 4 + y] = lw[inner, :, mine]
    wp[...] = lw[inner, :, other]
    for r in range(2):
        w_pair_send(r)
        w_nb_send(0, r)
    for r in range(2):
        w_zsend(0, r)
    for t in range(NT):
        x_send(t)
    cp_base.wait()
    quantize(0)
    w_pair_got(0)
    w_nb_send(1, 0)
    w_zsend(1, 0)
    w_nb_got(0, 0)
    w_zsend(2, 0)
    w_pair_got(1)
    w_nb_send(1, 1)
    w_fwd(0, 0)
    quantize(1)
    w_zsend(1, 1)
    w_nb_got(1, 0)
    w_zsend(3, 0)
    w_nb_got(0, 1)
    w_zsend(2, 1)
    w_fwd(0, 1)
    quantize(2)
    w_nb_got(1, 1)
    w_zsend(3, 1)
    w_fwd(1, 0)
    w_fwd(2, 0)
    for fi in range(FRAG):
        outer_core(fi)
    cp_t.wait()
    for c in range(NCH):
        targets_chunk(c)
    w_fwd(3, 0)
    w_fwd(1, 1)
    for p in range(4):
        w_end(p, 0)
    cp_x.wait()
    key_own(0)
    key_own(1)
    w_fwd(2, 1)
    x_got(0)
    key_pair(0, 0)
    key_pair(1, 0)
    w_fwd(3, 1)
    key_mid(0, 0)
    x_got(1)
    key_pair(0, 1)
    key_pair(1, 1)
    key_mid(1, 0)
    key_mid(0, 1)
    for p in range(4):
        w_end(p, 1)
    key_res(0, 0)
    key_pair(2, 0)
    key_pair(2, 1)
    key_mid(1, 1)
    key_own(2)
    key_res(0, 1)
    key_pair(3, 0)
    key_pair(3, 1)
    key_own(3)
    key_done(0)
    grad_unit(0)
    grad_unit(1)
    key_mid(2, 0)
    key_mid(2, 1)
    key_res(1, 0)
    key_res(1, 1)
    key_mid(3, 0)
    key_mid(3, 1)
    grad_fwd(0)
    key_done(1)
    grad_unit(2)
    grad_fwd(1)
    grad_ring(0)
    grad_unit(3)
    for fi in range(FRAG):
        outer_x(fi)
    key_res(2, 0)
    key_res(2, 1)
    grad_fwd(2)
    grad_ring(1)
    grad_pair(0)
    key_done(2)
    grad_unit(4)
    grad_fwd(3)
    grad_ring(2)
    grad_pair(1)
    grad_out(0)
    grad_unit(5)
    key_res(3, 0)
    key_res(3, 1)
    for fi in range(FRAG):
        outer_end(fi)
    grad_fwd(4)
    key_done(3)
    grad_unit(6)
    grad_ring(3)
    grad_pair(2)
    grad_out(1)
    grad_fwd(5)
    grad_unit(7)
    grad_ring(4)
    grad_pair(3)
    grad_out(2)
    grad_fwd(6)
    grad_ring(5)
    grad_pair(4)
    grad_out(3)
    grad_fwd(7)
    grad_ring(6)
    grad_pair(5)
    grad_out(4)
    grad_ring(7)
    grad_pair(6)
    grad_out(5)
    grad_pair(7)
    grad_out(6)
    grad_out(7)
    for c in started:
        c.wait_send()


def exchange(layer_order, own_layers, outer_base, tokens_in, target_keys):
    vm = pltpu.VMEM
    dma = pltpu.SemaphoreType.DMA
    anyspec = pl.BlockSpec(memory_space=pl.ANY)
    return pl.pallas_call(
        kernel,
        out_shape=(
            jax.ShapeDtypeStruct((64, 2 * HALF), BF),
            jax.ShapeDtypeStruct((FRAG, 64, 2 * HALF), BF),
        ),
        in_specs=[pl.BlockSpec(memory_space=pltpu.SMEM)] + [anyspec] * 4,
        out_specs=(pl.BlockSpec(memory_space=pltpu.VMEM), pl.BlockSpec(memory_space=pltpu.VMEM)),
        scratch_shapes=[
            vm((4, 64, 2 * HALF), BF),
            vm((FRAG, 64, 2 * HALF), BF),
            vm((512, 1024), BF),
            vm((NCH, 256, 512), BF),
            vm((2, 512, HALF), BF),
            vm((16, 64, HALF), BF),
            vm((64, HALF), BF),
            vm((NCH, NT, 256, TT), F32),
            vm((NCH, NT, 256, TT), BF),
            vm((NCH, NT, 256, TT), BF),
            vm((NCH, NT, 256, TT), BF),
            vm((NCH, NT, 256, TT), BF),
            vm((2, NCH, NT, 256, TT), BF),
            vm((16, 64, HALF), BF),
            vm((2, NU, 2, 16, QC), BF),
            vm((2, NU, 4, 16, QC), BF),
            vm((NU, 4, 16, QC), BF),
            vm((NU, 2, 16, QC), BF),
            vm((NU, 16, QC), BF),
            vm((NU, 16, QC), BF),
        ]
        + [vm((FRAG, 64, HALF), BF) for _ in range(7)]
        + [
            dma((4,)),
            dma((2, 4, 4)), dma((2, 4, 4)),
            dma((2,)), dma((2,)),
            dma((2, 2)), dma((2, 2)),
            dma((NT,)), dma((NT,)),
            dma((NCH, NT)), dma((NCH, NT)),
            dma((NCH, NT)), dma((NCH, NT)),
            dma((NCH, NT)), dma((NCH, NT)),
            dma((NU, 6)), dma((NU, 6)),
            dma((NU, 2)), dma((NU, 2)),
            dma((NU,)), dma((NU,)),
            dma((FRAG,)), dma((FRAG,)),
            dma((FRAG,)), dma((FRAG,)),
            dma((FRAG,)), dma((FRAG,)),
        ],
        compiler_params=pltpu.CompilerParams(
            collective_id=0, has_side_effects=True, vmem_limit_bytes=62 * 2**20
        ),
    )(layer_order, own_layers, outer_base, tokens_in, target_keys)


def per_device(local_weights, outer_base, momentum, layer_order, features, targets):
    grad, summed = exchange(layer_order, local_weights[0], outer_base, features[0], targets[0])
    mean_drift = summed.astype(F32) / lax.axis_size("island")
    moment_new = outer_mu * momentum + mean_drift
    base_new = (
        outer_base.astype(F32) + outer_rate * (mean_drift + outer_mu * moment_new)
    ).astype(BF)
    return (base_new, moment_new, grad.astype(F32)[None])


def solution(mesh):
    return jax.shard_map(
        per_device,
        mesh=mesh,
        in_specs=(
            P("island", None, "fsdp", "tp"),
            P(None, "fsdp", "tp"),
            P(None, "fsdp", "tp"),
            P(),
            P("island", "fsdp", "tp"),
            P("island", "fsdp", None),
        ),
        out_specs=(P(None, "fsdp", "tp"), P(None, "fsdp", "tp"), P("island", "fsdp", "tp")),
        check_vma=False,
    )
```

time: 377 us -> 150 us (0.40)
  waiting for transfers between devices: 274 us -> 0 us
  Pallas kernels: 0 us -> 139 us
  other arithmetic: 39.6 us -> 9.54 us
  matrix products: 24.4 us -> 0 us
  local copies, waits for them, and re-layouts: 21 us -> 0.01 us
  between operations: 15.7 us -> 0.65 us
    pallas_call x0 -> x1, Pallas kernels: none -> 139 us  [exchange(): pl.pallas_call(kernel, out_shape=(jax.ShapeDtypeStruct((64, 2 * HALF), BF...]
    psum x2 -> x0, waiting for transfers between devices: 130 us -> none  [the longest x1 90.5 us: per_device(): lax.psum(restored.astype(jnp.bfloat16), 'island').astype(jnp.float32)]
    reduce_scatter x1 -> x0, waiting for transfers between devices: 73.8 us -> none  [per_device(): lax.psum_scatter((lax.dot_general(residual, tokens_in, (((0,), (0,)), (()...]
    all_gather x1 -> x0, waiting for transfers between devices: 70.1 us -> none  [per_device(): lax.all_gather(inner_w, 'fsdp', axis=0, tiled=True)]
    dot_general x2 -> x0, matrix products: 24.4 us -> none  [the longest x1 12.3 us: per_device(): lax.dot_general(tokens_in, lax.all_gather(inner_w, 'fsdp', axis=0, tiled=...]
    convert_element_type x4 -> x1, other arithmetic: 17.6 us -> 8.29 us  [per_device(): base_new = (outer_base.astype(F32) + outer_rate * (mean_drift + outer_mu...]
    div x1 -> x0, local copies, waits for them, and re-layouts: 8.58 us -> none  [per_device(): summed.reshape(frag_n, rows_n, cols_n) / lax.axis_size('island')]
    sub x1 -> x0, local copies, waits for them, and re-layouts: 7.94 us -> none  [per_device(): drift = frag_layers.astype(jnp.float32) - base_f32]
  transfers between devices with their start and end apart: 4 -> 0, of which waited for: 4 -> 0; matrix products, arithmetic and copies ran while one was open for 18% -> 0% of each run, Pallas kernels for 0% -> 0%
where the time goes in v1:
time: 150 us
  Pallas kernels  139 us (93%)
  other arithmetic  9.54 us (6%)
    pallas_call x1, Pallas kernels, exchange(): pl.pallas_call(kernel, out_shape=(jax.ShapeDtypeStruct((64, 2 * HALF), BF...  139 us
    convert_element_type x1, other arithmetic, per_device(): base_new = (outer_base.astype(F32) + outer_rate * (mean_drift + outer_mu...  8.29 us

profile of v1, /device:TPU:8, one launch (start us, length us, event | category | flops | bytes accessed | tf_op | source)
XLA Modules:
  0.0 149.6 jit_solution(17466628299583358369)
XLA Ops:
  0.6 139.5 %shard_map.85 = (bf16[64,6144]{1,0:T(8,128)(2,1)}, bf16[3,64,6144]{2,1,0:T(8,128)(2,1)}) custom-call(s32[4]{0:T(128)} %lo_ref.1, bf16[4,64,6144]{2,1,0:T(8,128)(2,1)} %bitcast.7, bf16[3,64,6144]{2,1,0:T(8,128)(2,1)} %base_hbm.1, bf16[512,6144]{1,0:T(8,128)(2,1)} %bitcast.6, bf16[512,1024]{1,0:T(8,128)(2,1)} %bitcast.8), custom_call_target="tpu_custom_call" | custom-call | tf_op jit(solution)/shard_map/pallas_call | solution.py:429
  140.1 0.0 copy-start
  140.1 8.3 %add_convert_fusion = (bf16[3,64,6144]{2,1,0:T(8,128)(2,1)}, f32[3,64,6144]{2,1,0:T(8,128)}) fusion(bf16[3,64,6144]{2,1,0:T(8,128)(2,1)} %get-tuple-element.5, bf16[3,64,6144]{2,1,0:T(8,128)(2,1)} %base_hbm.1, f32[3,64,6144]{2,1,0:T(8,128)} %param.8), kind=kLoop, calls=%fused_computation | loop fusion | flops 11796480 | bytes 16515072 | tf_op jit(solution)/shard_map/convert_element_type | solution.py:488
  148.4 0.0 copy-done
  148.4 1.2 bitcast_convert_fusion
Async XLA Ops:
  140.1 8.3 %copy-start = (bf16[64,6144]{1,0:T(8,128)(2,1)S(1)}, bf16[64,6144]{1,0:T(8,128)(2,1)}, u32[]{:S(2)}) copy-start(bf16[64,6144]{1,0:T(8,128)(2,1)} %get-tuple-element.6) | copy-start | bytes 2359300

commit v2 on v1

--- a/solution.py
+++ b/solution.py
@@ -25,6 +25,7 @@
 QC = 1536
 NQ = HALF // QC
 NU = NCH * NQ
+NY = 3
 QT = 512
 
 
@@ -34,11 +35,11 @@
 
 def kernel(
     lo_ref, lw_hbm, base_hbm, x_hbm, t_hbm,
-    og_ref, os_ref,
-    lw, base, tt, tpm, xv, wv, wp, ka, kb, kr, ts, tr, rv, gv, r1, r2, sv, nr, uv, pr,
+    og_ref, os_hbm,
+    lw, base, tt, tpm, xv, wv, wp, ka, kb, kr, ts, tr, rv, gv, r1, r2, sv, nr, uv, pr, yb,
     qo, qs, qr, s2, xr, tot, fr,
-    loc_sem, wz_s, wz_r, wp_s, wp_r, wn_s, wn_r, x_s, x_r, kb_s, kb_r, tp_s, tp_r, rr_s, rr_r,
-    g_s, g_r, nb_s, nb_r, pr_s, pr_r, q_s, q_r, xl_s, xl_r, fr_s, fr_r,
+    loc_sem, os_sem, step_sem, wz_s, wz_r, wp_s, wp_r, wn_s, wn_r, x_s, x_r, kb_s, kb_r, tp_s, tp_r, rr_s, rr_r,
+    g_s, g_r, nb_s, nb_r, yb_s, yb_r, pr_s, pr_r, q_s, q_r, xl_s, xl_r, fr_s, fr_r,
 ):
     isl = lax.axis_index("island")
     f = lax.axis_index("fsdp")
@@ -51,8 +52,10 @@
     h = lax.rem(lax.div(yy + 1, 2), 2)
     yp = lax.rem(pp + core, 4)
     yn = lax.rem(3 - yy + core, 4)
-    ynp = lax.rem(3 - pp + core, 4)
-    yo = [y, yp, yn, ynp]
+    e = lax.rem(yy, 2)
+    slot_of = [e, 1 - e, 3 - e, 2 + e]
+    base_y = 2 * lax.div(yy, 2)
+    slot_y = [lax.rem(v + core, 4) for v in (base_y, base_y + 1, 2 - base_y, 3 - base_y)]
     zr = lax.rem(z + 1, 4)
     zl = lax.rem(z + 3, 4)
     z2 = lax.rem(z + 2, 4)
@@ -67,6 +70,10 @@
     mine = pl.ds(pl.multiple_of(h * HALF, HALF), HALF)
     other = pl.ds(pl.multiple_of((1 - h) * HALF, HALF), HALF)
 
+    barrier = pltpu.get_barrier_semaphore()
+    for dev in (d_pair, d_nb, d_right, d_left, d_tp, d_core, d_xlo):
+        pl.semaphore_signal(barrier, inc=1, device_id=dev, device_id_type=MESH)
+
     cp_lw = pltpu.make_async_copy(lw_hbm, lw, loc_sem.at[0])
     cp_lw.start()
     cp_base = pltpu.make_async_copy(base_hbm, base, loc_sem.at[1])
@@ -76,9 +83,10 @@
     cp_t = pltpu.make_async_copy(t_hbm, tt, loc_sem.at[3])
     cp_t.start()
 
-    barrier = pltpu.get_barrier_semaphore()
-    for dev in (d_pair, d_nb, d_right, d_left, d_tp, d_core, d_xlo):
-        pl.semaphore_signal(barrier, inc=1, device_id=dev, device_id_type=MESH)
+    cp_lw.wait()
+    inner = lo_ref[FRAG]
+    wv[z, e] = lw[inner, :, mine]
+    wp[...] = lw[inner, :, other]
     pl.semaphore_wait(barrier, 7)
 
     started = []
@@ -97,7 +105,7 @@
         copy(dst, dst, ss, rs, dev).wait_recv()
 
     def wslot(zo, p, lo, n):
-        return wv.at[zo * 4 + yo[p], pl.ds(lo, n)]
+        return wv.at[zo, slot_of[p], pl.ds(lo, n)]
 
     def w_zsend(p, r):
         piece = wslot(z, p, r * 32, 32)
@@ -121,7 +129,8 @@
 
     def w_nb_send(p, r):
         piece = wslot(z, p, r * 32, 32)
-        send(piece, piece, wn_s.at[p, r], wn_r.at[p, r], d_nb)
+        there = wv.at[z, 2 + slot_of[p], pl.ds(r * 32, 32)]
+        send(piece, there, wn_s.at[p, r], wn_r.at[p, r], d_nb)
 
     def w_pair_got(r):
         wait_recv(wslot(z, 1, r * 32, 32), wp_s.at[r], wp_r.at[r], d_pair)
@@ -137,7 +146,7 @@
         wait_recv(xv.at[1, pl.ds(t * TT, TT)], x_s.at[t], x_r.at[t], d_pair)
 
     def chunk_w(c):
-        return wv[:, pl.ds(c * 16, 16), :].reshape(256, HALF)
+        return wv[:, :, pl.ds(c * 16, 16), :].reshape(256, HALF)
 
     def key_own(c):
         for t in range(NT):
@@ -168,12 +177,18 @@
         row = lax.broadcasted_iota(jnp.int32, (256, 1024), 0)
         col = lax.broadcasted_iota(jnp.int32, (256, 1024), 1)
         slot = row >> 4
-        want = ((slot & 3) * 4 + (slot >> 2)) * 64 + c * 16 + (row & 15)
+        p = slot & 3
+        owner_y = jnp.where(p < 2, jnp.where(p == 0, slot_y[0], slot_y[1]), jnp.where(p == 2, slot_y[2], slot_y[3]))
+        want = (owner_y * 4 + (slot >> 2)) * 64 + c * 16 + (row & 15)
         pick = jnp.where(col == want, 1.0, 0.0).astype(BF)
         tpm[c] = nt_dot(pick, tt[...]).astype(BF)
 
-    def gpart(zo, lo, n, c, q):
-        return gv.at[pl.ds(zo * 4 + lo, n), pl.ds(c * 16, 16), pl.ds(q * QC, QC)]
+    def gcut(zo, lo, n, u):
+        c, q = u // NQ, u % NQ
+        return zo, pl.ds(lo, n), pl.ds(c * 16, 16), pl.ds(q * QC, QC)
+
+    def late(u):
+        return u >= NU - NY
 
     def grad_unit(u):
         c, q = u // NQ, u % NQ
@@ -188,77 +203,104 @@
                         rv[i, c, t], xv[i, pl.ds(t * TT, TT), cols], preferred_element_type=F32
                     )
                     acc = part if acc is None else acc + part
-            gv[:, pl.ds(c * 16, 16), cols] = (acc * KEY_SCALE).astype(BF).reshape(16, 16, 512)
-
-        send(gpart(z2, 0, 2, c, q), r1.at[0, u], g_s.at[u, 0], g_r.at[u, 0], d_right)
-        send(gpart(z2, 2, 2, c, q), r1.at[1, u], g_s.at[u, 1], g_r.at[u, 1], d_left)
-        send(gpart(zr, 2, 2, c, q), r2.at[0, u, pl.ds(2, 2)], g_s.at[u, 2], g_r.at[u, 2], d_right)
-        send(gpart(zl, 0, 2, c, q), r2.at[1, u, pl.ds(0, 2)], g_s.at[u, 3], g_r.at[u, 3], d_left)
+            gv[:, :, pl.ds(c * 16, 16), cols] = (acc * KEY_SCALE).astype(BF).reshape(4, 4, 16, 512)
+
+        if late(u):
+            src = gv.at[:, pl.ds(2, 2), pl.ds(c * 16, 16), pl.ds(q * QC, QC)]
+            v = u - (NU - NY)
+            send(src, yb.at[v], yb_s.at[v], yb_r.at[v], d_nb)
+        else:
+            grad_start(u, 2)
+
+    def grad_start(u, n):
+        lo, hi = pl.ds(0, n), pl.ds(n, n)
+        send(gv.at[gcut(z2, 0, n, u)], r1.at[0, u, lo], g_s.at[u, 0], g_r.at[u, 0], d_right)
+        send(gv.at[gcut(z2, n, n, u)], r1.at[1, u, lo], g_s.at[u, 1], g_r.at[u, 1], d_left)
+        send(gv.at[gcut(zr, n, n, u)], r2.at[0, u, hi], g_s.at[u, 2], g_r.at[u, 2], d_right)
+        send(gv.at[gcut(zl, 0, n, u)], r2.at[1, u, lo], g_s.at[u, 3], g_r.at[u, 3], d_left)
+
+    def grad_nb(u):
+        if not late(u):
+            return
+        c, q = u // NQ, u % NQ
+        v = u - (NU - NY)
+        wait_recv(yb.at[v], yb_s.at[v], yb_r.at[v], d_nb)
+        for zo in range(4):
+            cut = gcut(zo, 0, 2, u)
+            gv[cut] = (gv[cut].astype(F32) + yb[v, zo].astype(F32)).astype(BF)
+        grad_start(u, 1)
 
     def grad_fwd(u):
+        n = 1 if late(u) else 2
+        lo, hi = pl.ds(0, n), pl.ds(n, n)
+        wait_recv(r1.at[0, u, lo], g_s.at[u, 0], g_r.at[u, 0], d_right)
+        cut = gcut(zr, 0, n, u)
+        gv[cut] = (gv[cut].astype(F32) + r1[0, u, 0:n].astype(F32)).astype(BF)
+        send(gv.at[cut], r2.at[0, u, lo], g_s.at[u, 4], g_r.at[u, 4], d_right)
+        wait_recv(r1.at[1, u, lo], g_s.at[u, 1], g_r.at[u, 1], d_left)
+        cut = gcut(zl, n, n, u)
+        gv[cut] = (gv[cut].astype(F32) + r1[1, u, 0:n].astype(F32)).astype(BF)
+        send(gv.at[cut], r2.at[1, u, hi], g_s.at[u, 5], g_r.at[u, 5], d_left)
+
+    def grad_ring(u):
+        n = 1 if late(u) else 2
+        lo, hi = pl.ds(0, n), pl.ds(n, n)
+        wait_recv(r2.at[0, u, hi], g_s.at[u, 2], g_r.at[u, 2], d_right)
+        wait_recv(r2.at[1, u, lo], g_s.at[u, 3], g_r.at[u, 3], d_left)
+        wait_recv(r2.at[0, u, lo], g_s.at[u, 4], g_r.at[u, 4], d_right)
+        wait_recv(r2.at[1, u, hi], g_s.at[u, 5], g_r.at[u, 5], d_left)
+        own = gv[gcut(z, 0, 2 * n, u)].astype(F32)
+        own = own + r2[0, u, 0:2 * n].astype(F32) + r2[1, u, 0:2 * n].astype(F32)
+        if late(u):
+            sv[u, 0:2] = own.astype(BF)
+            send(sv.at[u, 1 - e], pr.at[u], pr_s.at[u], pr_r.at[u], d_pair)
+            grad_store(u, h, sv[u, e])
+        else:
+            sv[u] = own.astype(BF)
+            send(sv.at[u, pl.ds(2, 2)], nr.at[u], nb_s.at[u], nb_r.at[u], d_nb)
+
+    def grad_store(u, side, value):
         c, q = u // NQ, u % NQ
-        rows, cols = pl.ds(c * 16, 16), pl.ds(q * QC, QC)
-        wait_recv(r1.at[0, u], g_s.at[u, 0], g_r.at[u, 0], d_right)
-        sl = pl.ds(zr * 4, 2)
-        gv[sl, rows, cols] = (gv[sl, rows, cols].astype(F32) + r1[0, u].astype(F32)).astype(BF)
-        send(gpart(zr, 0, 2, c, q), r2.at[0, u, pl.ds(0, 2)], g_s.at[u, 4], g_r.at[u, 4], d_right)
-        wait_recv(r1.at[1, u], g_s.at[u, 1], g_r.at[u, 1], d_left)
-        sl2 = pl.ds(zl * 4 + 2, 2)
-        gv[sl2, rows, cols] = (gv[sl2, rows, cols].astype(F32) + r1[1, u].astype(F32)).astype(BF)
-        send(gpart(zl, 2, 2, c, q), r2.at[1, u, pl.ds(2, 2)], g_s.at[u, 5], g_r.at[u, 5], d_left)
-
-    def grad_ring(u):
-        c, q = u // NQ, u % NQ
-        wait_recv(r2.at[0, u, pl.ds(2, 2)], g_s.at[u, 2], g_r.at[u, 2], d_right)
-        wait_recv(r2.at[1, u, pl.ds(0, 2)], g_s.at[u, 3], g_r.at[u, 3], d_left)
-        wait_recv(r2.at[0, u, pl.ds(0, 2)], g_s.at[u, 4], g_r.at[u, 4], d_right)
-        wait_recv(r2.at[1, u, pl.ds(2, 2)], g_s.at[u, 5], g_r.at[u, 5], d_left)
-        own = gv[pl.ds(z * 4, 4), pl.ds(c * 16, 16), pl.ds(q * QC, QC)].astype(F32)
-        sv[u] = (own + r2[0, u].astype(F32) + r2[1, u].astype(F32)).astype(BF)
-        send(sv.at[u, yn], nr.at[u, 0], nb_s.at[u, 0], nb_r.at[u, 0], d_nb)
-        send(sv.at[u, ynp], nr.at[u, 1], nb_s.at[u, 1], nb_r.at[u, 1], d_nb)
+        cols = pl.ds(pl.multiple_of(side * HALF + q * QC, QC), QC)
+        og_ref[c * 16:(c + 1) * 16, cols] = value
 
     def grad_pair(u):
-        c, q = u // NQ, u % NQ
-        wait_recv(nr.at[u, 1], nb_s.at[u, 1], nb_r.at[u, 1], d_nb)
-        uv[u] = (sv[u, yp].astype(F32) + nr[u, 1].astype(F32)).astype(BF)
+        if late(u):
+            return
+        wait_recv(nr.at[u], nb_s.at[u], nb_r.at[u], d_nb)
+        uv[u] = (sv[u, 1 - e].astype(F32) + nr[u, 1 - e].astype(F32)).astype(BF)
         send(uv.at[u], pr.at[u], pr_s.at[u], pr_r.at[u], d_pair)
-        wait_recv(nr.at[u, 0], nb_s.at[u, 0], nb_r.at[u, 0], d_nb)
-        cols = pl.ds(pl.multiple_of(h * HALF + q * QC, QC), QC)
-        og_ref[c * 16:(c + 1) * 16, cols] = (sv[u, y].astype(F32) + nr[u, 0].astype(F32)).astype(BF)
+        grad_store(u, h, (sv[u, e].astype(F32) + nr[u, e].astype(F32)).astype(BF))
 
     def grad_out(u):
-        c, q = u // NQ, u % NQ
         wait_recv(pr.at[u], pr_s.at[u], pr_r.at[u], d_pair)
-        cols = pl.ds(pl.multiple_of((1 - h) * HALF + q * QC, QC), QC)
-        og_ref[c * 16:(c + 1) * 16, cols] = pr[u]
+        grad_store(u, 1 - h, pr[u])
 
     sel_r = lax.broadcasted_iota(jnp.int32, (128, 128), 0)
     sel_c = lax.broadcasted_iota(jnp.int32, (128, 128), 1)
 
-    def quantize(fi):
+    def quantize(fi, own):
         layer = lo_ref[fi]
-
-        def half_of(side, dst):
-            @pl.loop(0, HALF // QT)
-            def _(j):
-                pick = jnp.where(sel_r == (sel_c | (QB - 1)), 1.0, 0.0).astype(BF)
-                for k in range(QT // 128):
-                    col = pl.multiple_of(side * HALF + j * QT + k * 128, 128)
-                    a = lw[layer, :, pl.ds(col, 128)].astype(F32)
-                    b = base[fi, :, pl.ds(col, 128)].astype(F32)
-                    drift = a - b
-                    m = jnp.abs(drift)
-                    for s in (1, 2, 4, 8, 16):
-                        m = jnp.maximum(m, pltpu.roll(m, s, 1))
-                    sc = jnp.dot((m + scale_eps).astype(BF), pick, preferred_element_type=F32)
-                    quant = (drift / sc).astype(BF).astype(F32)
-                    out = pl.multiple_of(j * QT + k * 128, 128)
-                    dst[fi, :, pl.ds(out, 128)] = (quant * sc).astype(BF)
-
-        half_of(1 - core, qs)
-        send(qs.at[fi], qr.at[fi], q_s.at[fi], q_r.at[fi], d_core)
-        half_of(core, qo)
+        side, dst = (core, qo) if own else (1 - core, qs)
+
+        @pl.loop(0, HALF // QT)
+        def _(j):
+            pick = jnp.where(sel_r == (sel_c | (QB - 1)), 1.0, 0.0).astype(BF)
+            for k in range(QT // 128):
+                col = pl.multiple_of(side * HALF + j * QT + k * 128, 128)
+                a = lw[layer, :, pl.ds(col, 128)].astype(F32)
+                b = base[fi, :, pl.ds(col, 128)].astype(F32)
+                drift = a - b
+                m = jnp.abs(drift)
+                for s in (1, 2, 4, 8, 16):
+                    m = jnp.maximum(m, pltpu.roll(m, s, 1))
+                sc = jnp.dot((m + scale_eps).astype(BF), pick, preferred_element_type=F32)
+                quant = (drift / sc).astype(BF).astype(F32)
+                out = pl.multiple_of(j * QT + k * 128, 128)
+                dst[fi, :, pl.ds(out, 128)] = (quant * sc).astype(BF)
+
+        if not own:
+            send(qs.at[fi], qr.at[fi], q_s.at[fi], q_r.at[fi], d_core)
 
     def tiles(body):
         @pl.loop(0, HALF // QT)
@@ -278,25 +320,28 @@
         wait_recv(xr.at[fi], xl_s.at[fi], xl_r.at[fi], d_xlo)
 
         def body(cols, j):
-            v = (s2[fi, :, cols].astype(F32) + xr[fi, :, cols].astype(F32)).astype(BF)
-            tot[fi, :, cols] = v
-            os_ref[fi, :, pl.ds(pl.multiple_of(core * HALF + j * QT, QT), QT)] = v
+            tot[fi, :, cols] = (s2[fi, :, cols].astype(F32) + xr[fi, :, cols].astype(F32)).astype(BF)
 
         tiles(body)
         send(tot.at[fi], fr.at[fi], fr_s.at[fi], fr_r.at[fi], d_core)
+        write_sum(tot, fi, core, 0)
+
+    def write_sum(src, fi, side, k):
+        cols = pl.ds(pl.multiple_of(side * HALF, HALF), HALF)
+        c = pltpu.make_async_copy(src.at[fi], os_hbm.at[fi, :, cols], os_sem.at[fi, k])
+        c.start()
+        written.append(c)
 
     def outer_end(fi):
         wait_recv(fr.at[fi], fr_s.at[fi], fr_r.at[fi], d_core)
-
-        def body(cols, j):
-            os_ref[fi, :, pl.ds(pl.multiple_of((1 - core) * HALF + j * QT, QT), QT)] = fr[fi, :, cols]
-
-        tiles(body)
-
-    cp_lw.wait()
-    inner = lo_ref[FRAG]
-    wv[z * 4 + y] = lw[inner, :, mine]
-    wp[...] = lw[inner, :, other]
+        write_sum(fr, fi, 1 - core, 1)
+
+    written = []
+
+    def in_step():
+        pl.semaphore_signal(step_sem, inc=1, device_id=d_core, device_id_type=MESH)
+        pl.semaphore_wait(step_sem, 1)
+
     for r in range(2):
         w_pair_send(r)
         w_nb_send(0, r)
@@ -305,7 +350,8 @@
     for t in range(NT):
         x_send(t)
     cp_base.wait()
-    quantize(0)
+    quantize(0, False)
+    quantize(0, True)
     w_pair_got(0)
     w_nb_send(1, 0)
     w_zsend(1, 0)
@@ -314,14 +360,16 @@
     w_pair_got(1)
     w_nb_send(1, 1)
     w_fwd(0, 0)
-    quantize(1)
+    quantize(1, False)
+    quantize(1, True)
     w_zsend(1, 1)
     w_nb_got(1, 0)
     w_zsend(3, 0)
     w_nb_got(0, 1)
     w_zsend(2, 1)
     w_fwd(0, 1)
-    quantize(2)
+    quantize(2, False)
+    quantize(2, True)
     w_nb_got(1, 1)
     w_zsend(3, 1)
     w_fwd(1, 0)
@@ -361,63 +409,74 @@
     key_pair(3, 1)
     key_own(3)
     key_done(0)
+    in_step()
     grad_unit(0)
-    grad_unit(1)
     key_mid(2, 0)
     key_mid(2, 1)
     key_res(1, 0)
     key_res(1, 1)
+    in_step()
+    grad_unit(1)
     key_mid(3, 0)
     key_mid(3, 1)
     grad_fwd(0)
     key_done(1)
+    in_step()
     grad_unit(2)
+    key_res(2, 0)
+    key_res(2, 1)
     grad_fwd(1)
     grad_ring(0)
+    outer_x(0)
+    key_res(3, 0)
+    key_res(3, 1)
+    in_step()
     grad_unit(3)
-    for fi in range(FRAG):
-        outer_x(fi)
-    key_res(2, 0)
-    key_res(2, 1)
+    key_done(2)
     grad_fwd(2)
     grad_ring(1)
     grad_pair(0)
-    key_done(2)
+    in_step()
+    grad_unit(5)
     grad_unit(4)
+    outer_x(1)
+    key_done(3)
     grad_fwd(3)
     grad_ring(2)
     grad_pair(1)
     grad_out(0)
-    grad_unit(5)
-    key_res(3, 0)
-    key_res(3, 1)
-    for fi in range(FRAG):
-        outer_end(fi)
+    in_step()
+    grad_unit(6)
+    grad_unit(7)
+    outer_x(2)
+    grad_nb(5)
     grad_fwd(4)
-    key_done(3)
-    grad_unit(6)
     grad_ring(3)
     grad_pair(2)
     grad_out(1)
+    in_step()
+    grad_nb(6)
     grad_fwd(5)
-    grad_unit(7)
     grad_ring(4)
     grad_pair(3)
     grad_out(2)
+    for fi in range(FRAG):
+        outer_end(fi)
+    in_step()
+    grad_nb(7)
     grad_fwd(6)
     grad_ring(5)
     grad_pair(4)
     grad_out(3)
     grad_fwd(7)
     grad_ring(6)
-    grad_pair(5)
     grad_out(4)
+    grad_out(5)
     grad_ring(7)
-    grad_pair(6)
-    grad_out(5)
-    grad_pair(7)
     grad_out(6)
     grad_out(7)
+    for c in written:
+        c.wait()
     for c in started:
         c.wait_send()
 
@@ -433,14 +492,14 @@
             jax.ShapeDtypeStruct((FRAG, 64, 2 * HALF), BF),
         ),
         in_specs=[pl.BlockSpec(memory_space=pltpu.SMEM)] + [anyspec] * 4,
-        out_specs=(pl.BlockSpec(memory_space=pltpu.VMEM), pl.BlockSpec(memory_space=pltpu.VMEM)),
+        out_specs=(pl.BlockSpec(memory_space=pltpu.VMEM), anyspec),
         scratch_shapes=[
             vm((4, 64, 2 * HALF), BF),
             vm((FRAG, 64, 2 * HALF), BF),
             vm((512, 1024), BF),
             vm((NCH, 256, 512), BF),
             vm((2, 512, HALF), BF),
-            vm((16, 64, HALF), BF),
+            vm((4, 4, 64, HALF), BF),
             vm((64, HALF), BF),
             vm((NCH, NT, 256, TT), F32),
             vm((NCH, NT, 256, TT), BF),
@@ -448,17 +507,18 @@
             vm((NCH, NT, 256, TT), BF),
             vm((NCH, NT, 256, TT), BF),
             vm((2, NCH, NT, 256, TT), BF),
-            vm((16, 64, HALF), BF),
+            vm((4, 4, 64, HALF), BF),
             vm((2, NU, 2, 16, QC), BF),
             vm((2, NU, 4, 16, QC), BF),
             vm((NU, 4, 16, QC), BF),
             vm((NU, 2, 16, QC), BF),
             vm((NU, 16, QC), BF),
             vm((NU, 16, QC), BF),
+            vm((NY, 4, 2, 16, QC), BF),
         ]
         + [vm((FRAG, 64, HALF), BF) for _ in range(7)]
         + [
-            dma((4,)),
+            dma((4,)), dma((FRAG, 2)), pltpu.SemaphoreType.REGULAR,
             dma((2, 4, 4)), dma((2, 4, 4)),
             dma((2,)), dma((2,)),
             dma((2, 2)), dma((2, 2)),
@@ -467,7 +527,8 @@
             dma((NCH, NT)), dma((NCH, NT)),
             dma((NCH, NT)), dma((NCH, NT)),
             dma((NU, 6)), dma((NU, 6)),
-            dma((NU, 2)), dma((NU, 2)),
+            dma((NU,)), dma((NU,)),
+            dma((NY,)), dma((NY,)),
             dma((NU,)), dma((NU,)),
             dma((FRAG,)), dma((FRAG,)),
             dma((FRAG,)), dma((FRAG,)),

time: 150 us -> 144 us (0.960)
  Pallas kernels: 139 us -> 132 us
    pallas_call x1, Pallas kernels: 139 us -> 132 us  [exchange(): pl.pallas_call(kernel, out_shape=(jax.ShapeDtypeStruct((64, 2 * HALF), BF...]
where the time goes in v2:
time: 144 us; the launch traced here: 142 us
  Pallas kernels  132 us (92%)
  other arithmetic  9.54 us (7%)
    pallas_call x1, Pallas kernels, exchange(): pl.pallas_call(kernel, out_shape=(jax.ShapeDtypeStruct((64, 2 * HALF), BF...  132 us
    convert_element_type x1, other arithmetic, per_device(): base_new = (outer_base.astype(F32) + outer_rate * (mean_drift + outer_mu...  8.29 us

profile of v2, /device:TPU:8, one launch (start us, length us, event | category | flops | bytes accessed | tf_op | source)
XLA Modules:
  0.0 142.5 jit_solution(15931656038381306709)
XLA Ops:
  0.6 132.3 %shard_map.85 = (bf16[64,6144]{1,0:T(8,128)(2,1)}, bf16[3,64,6144]{2,1,0:T(8,128)(2,1)}) custom-call(s32[4]{0:T(128)} %lo_ref.1, bf16[4,64,6144]{2,1,0:T(8,128)(2,1)} %bitcast.7, bf16[3,64,6144]{2,1,0:T(8,128)(2,1)} %base_hbm.1, bf16[512,6144]{1,0:T(8,128)(2,1)} %bitcast.6, bf16[512,1024]{1,0:T(8,128)(2,1)} %bitcast.8), custom_call_target="tpu_custom_call" | custom-call | tf_op jit(solution)/shard_map/pallas_call | solution.py:488
  132.9 0.0 copy-start
  132.9 8.3 %add_convert_fusion = (bf16[3,64,6144]{2,1,0:T(8,128)(2,1)}, f32[3,64,6144]{2,1,0:T(8,128)}) fusion(bf16[3,64,6144]{2,1,0:T(8,128)(2,1)} %get-tuple-element.5, bf16[3,64,6144]{2,1,0:T(8,128)(2,1)} %base_hbm.1, f32[3,64,6144]{2,1,0:T(8,128)} %param.8), kind=kLoop, calls=%fused_computation | loop fusion | flops 11796480 | bytes 16515072 | tf_op jit(solution)/shard_map/convert_element_type | solution.py:549
  141.2 0.0 copy-done
  141.2 1.2 bitcast_convert_fusion
Async XLA Ops:
  132.9 8.3 %copy-start = (bf16[64,6144]{1,0:T(8,128)(2,1)S(1)}, bf16[64,6144]{1,0:T(8,128)(2,1)}, u32[]{:S(2)}) copy-start(bf16[64,6144]{1,0:T(8,128)(2,1)} %get-tuple-element.6) | copy-start | bytes 2359300

commit v3 on v2

--- a/solution.py
+++ b/solution.py
@@ -36,9 +36,9 @@
 def kernel(
     lo_ref, lw_hbm, base_hbm, x_hbm, t_hbm,
     og_ref, os_hbm,
-    lw, base, tt, tpm, xv, wv, wp, ka, kb, kr, ts, tr, rv, gv, r1, r2, sv, nr, uv, pr, yb,
-    qo, qs, qr, s2, xr, tot, fr,
-    loc_sem, os_sem, step_sem, wz_s, wz_r, wp_s, wp_r, wn_s, wn_r, x_s, x_r, kb_s, kb_r, tp_s, tp_r, rr_s, rr_r,
+    tt, tpm, xv, wv, wp, ka, kb, kr, ts, tr, rv, gv, r1, r2, sv, nr, uv, pr, yb,
+    qo, qs, qr, s2, xr, fr,
+    loc_sem, load_sem, os_sem, step_sem, wz_s, wz_r, wp_s, wp_r, wn_s, wn_r, x_s, x_r, kb_s, kb_r, tp_s, tp_r, rr_s, rr_r,
     g_s, g_r, nb_s, nb_r, yb_s, yb_r, pr_s, pr_r, q_s, q_r, xl_s, xl_r, fr_s, fr_r,
 ):
     isl = lax.axis_index("island")
@@ -74,19 +74,28 @@
     for dev in (d_pair, d_nb, d_right, d_left, d_tp, d_core, d_xlo):
         pl.semaphore_signal(barrier, inc=1, device_id=dev, device_id_type=MESH)
 
-    cp_lw = pltpu.make_async_copy(lw_hbm, lw, loc_sem.at[0])
-    cp_lw.start()
-    cp_base = pltpu.make_async_copy(base_hbm, base, loc_sem.at[1])
-    cp_base.start()
+    loads = []
+
+    def load(src, n, first, count):
+        for layer in range(count):
+            for side in range(2):
+                cut = src.at[layer, :, pl.ds(side * HALF, HALF)]
+                c = pltpu.make_async_copy(cut, gv.at[layer, first + side], load_sem.at[n, layer, side])
+                c.start()
+                loads.append(c)
+
+    load(lw_hbm, 0, 0, 4)
     cp_x = pltpu.make_async_copy(x_hbm.at[:, mine], xv.at[0], loc_sem.at[2])
     cp_x.start()
     cp_t = pltpu.make_async_copy(t_hbm, tt, loc_sem.at[3])
     cp_t.start()
 
-    cp_lw.wait()
+    for c in loads:
+        c.wait()
     inner = lo_ref[FRAG]
-    wv[z, e] = lw[inner, :, mine]
-    wp[...] = lw[inner, :, other]
+    wv[z, e] = gv[inner, h]
+    wp[...] = gv[inner, 1 - h]
+    load(base_hbm, 1, 2, FRAG)
     pl.semaphore_wait(barrier, 7)
 
     started = []
@@ -287,17 +296,16 @@
         def _(j):
             pick = jnp.where(sel_r == (sel_c | (QB - 1)), 1.0, 0.0).astype(BF)
             for k in range(QT // 128):
-                col = pl.multiple_of(side * HALF + j * QT + k * 128, 128)
-                a = lw[layer, :, pl.ds(col, 128)].astype(F32)
-                b = base[fi, :, pl.ds(col, 128)].astype(F32)
+                col = pl.ds(pl.multiple_of(j * QT + k * 128, 128), 128)
+                a = gv[layer, side, :, col].astype(F32)
+                b = gv[fi, 2 + side, :, col].astype(F32)
                 drift = a - b
                 m = jnp.abs(drift)
                 for s in (1, 2, 4, 8, 16):
                     m = jnp.maximum(m, pltpu.roll(m, s, 1))
                 sc = jnp.dot((m + scale_eps).astype(BF), pick, preferred_element_type=F32)
                 quant = (drift / sc).astype(BF).astype(F32)
-                out = pl.multiple_of(j * QT + k * 128, 128)
-                dst[fi, :, pl.ds(out, 128)] = (quant * sc).astype(BF)
+                dst[fi, :, col] = (quant * sc).astype(BF)
 
         if not own:
             send(qs.at[fi], qr.at[fi], q_s.at[fi], q_r.at[fi], d_core)
@@ -320,11 +328,11 @@
         wait_recv(xr.at[fi], xl_s.at[fi], xl_r.at[fi], d_xlo)
 
         def body(cols, j):
-            tot[fi, :, cols] = (s2[fi, :, cols].astype(F32) + xr[fi, :, cols].astype(F32)).astype(BF)
+            qo[fi, :, cols] = (s2[fi, :, cols].astype(F32) + xr[fi, :, cols].astype(F32)).astype(BF)
 
         tiles(body)
-        send(tot.at[fi], fr.at[fi], fr_s.at[fi], fr_r.at[fi], d_core)
-        write_sum(tot, fi, core, 0)
+        send(qo.at[fi], fr.at[fi], fr_s.at[fi], fr_r.at[fi], d_core)
+        write_sum(qo, fi, core, 0)
 
     def write_sum(src, fi, side, k):
         cols = pl.ds(pl.multiple_of(side * HALF, HALF), HALF)
@@ -349,7 +357,8 @@
         w_zsend(0, r)
     for t in range(NT):
         x_send(t)
-    cp_base.wait()
+    for c in loads[8:]:
+        c.wait()
     quantize(0, False)
     quantize(0, True)
     w_pair_got(0)
@@ -392,29 +401,29 @@
     key_pair(1, 0)
     w_fwd(3, 1)
     key_mid(0, 0)
+    key_mid(1, 0)
     x_got(1)
     key_pair(0, 1)
     key_pair(1, 1)
-    key_mid(1, 0)
+    key_res(0, 0)
     key_mid(0, 1)
     for p in range(4):
         w_end(p, 1)
-    key_res(0, 0)
     key_pair(2, 0)
+    key_mid(1, 1)
+    key_res(0, 1)
     key_pair(2, 1)
-    key_mid(1, 1)
     key_own(2)
-    key_res(0, 1)
+    key_res(1, 0)
+    key_done(0)
+    in_step()
+    grad_unit(0)
     key_pair(3, 0)
     key_pair(3, 1)
-    key_own(3)
-    key_done(0)
-    in_step()
-    grad_unit(0)
     key_mid(2, 0)
     key_mid(2, 1)
-    key_res(1, 0)
     key_res(1, 1)
+    key_own(3)
     in_step()
     grad_unit(1)
     key_mid(3, 0)
@@ -494,8 +503,6 @@
         in_specs=[pl.BlockSpec(memory_space=pltpu.SMEM)] + [anyspec] * 4,
         out_specs=(pl.BlockSpec(memory_space=pltpu.VMEM), anyspec),
         scratch_shapes=[
-            vm((4, 64, 2 * HALF), BF),
-            vm((FRAG, 64, 2 * HALF), BF),
             vm((512, 1024), BF),
             vm((NCH, 256, 512), BF),
             vm((2, 512, HALF), BF),
@@ -516,9 +523,9 @@
             vm((NU, 16, QC), BF),
             vm((NY, 4, 2, 16, QC), BF),
         ]
-        + [vm((FRAG, 64, HALF), BF) for _ in range(7)]
+        + [vm((FRAG, 64, HALF), BF) for _ in range(6)]
         + [
-            dma((4,)), dma((FRAG, 2)), pltpu.SemaphoreType.REGULAR,
+            dma((4,)), dma((2, 4, 2)), dma((FRAG, 2)), pltpu.SemaphoreType.REGULAR,
             dma((2, 4, 4)), dma((2, 4, 4)),
             dma((2,)), dma((2,)),
             dma((2, 2)), dma((2, 2)),
@@ -535,7 +542,7 @@
             dma((FRAG,)), dma((FRAG,)),
         ],
         compiler_params=pltpu.CompilerParams(
-            collective_id=0, has_side_effects=True, vmem_limit_bytes=62 * 2**20
+            collective_id=0, has_side_effects=True, vmem_limit_bytes=48 * 2**20
         ),
     )(layer_order, own_layers, outer_base, tokens_in, target_keys)
 

time: 144 us -> 142 us (0.986)
  other arithmetic: 9.54 us -> 5.67 us
  local copies, waits for them, and re-layouts: 0.01 us -> 1.88 us
    convert_element_type x1, other arithmetic: 8.29 us -> 4.42 us  [per_device(): base_new = (outer_base.astype(F32) + outer_rate * (mean_drift + outer_mu...]
    unnamed x2 -> x8, local copies, waits for them, and re-layouts: 0.01 us -> 1.88 us
where the time goes in v3:
time: 142 us; the launch traced here: 141 us
  Pallas kernels  133 us (94%)
  other arithmetic  5.67 us (4%)
  local copies, waits for them, and re-layouts  1.88 us (1%)
    pallas_call x1, Pallas kernels, exchange(): pl.pallas_call(kernel, out_shape=(jax.ShapeDtypeStruct((64, 2 * HALF), BF...  133 us
    convert_element_type x1, other arithmetic, per_device(): base_new = (outer_base.astype(F32) + outer_rate * (mean_drift + outer_mu...  4.42 us

profile of v3, /device:TPU:8, one launch (start us, length us, event | category | flops | bytes accessed | tf_op | source)
XLA Modules:
  0.0 141.4 jit_solution(12615013981239839753)
XLA Ops:
  0.6 0.0 copy-start
  0.6 1.2 copy-done
  1.9 0.0 copy-start.1
  1.9 0.7 copy-done.1
  2.5 0.0 copy-start.2
  2.5 0.0 copy-start.3
  2.5 133.1 %shard_map.85 = (bf16[64,6144]{1,0:T(8,128)(2,1)S(1)}, bf16[3,64,6144]{2,1,0:T(8,128)(2,1)S(1)}) custom-call(s32[4]{0:T(128)S(1)} %copy-done.1, bf16[4,64,6144]{2,1,0:T(8,128)(2,1)} %bitcast.8, bf16[3,64,6144]{2,1,0:T(8,128)(2,1)} %base_hbm.1, bf16[512,6144]{1,0:T(8,128)(2,1)} %bitcast.7, bf16[512,1024]{1,0:T(8,128)(2,1)S(1)} %bitcast.6), custom_call_target="tpu_custom_call" | custom-call | tf_op jit(solution)/shard_map/pallas_call | solution.py:497
  135.7 0.0 copy-done.2
  135.7 0.0 copy-done.3
  135.7 4.4 %add_convert_fusion = (bf16[3,64,6144]{2,1,0:T(8,128)(2,1)}, f32[3,64,6144]{2,1,0:T(8,128)}) fusion(bf16[3,64,6144]{2,1,0:T(8,128)(2,1)S(1)} %get-tuple-element.5, bf16[3,64,6144]{2,1,0:T(8,128)(2,1)S(1)} %copy-done.2, f32[3,64,6144]{2,1,0:T(8,128)S(1)} %copy-done.3), kind=kLoop, calls=%fused_computation | loop fusion | flops 11796480 | bytes 16515072 | tf_op jit(solution)/shard_map/convert_element_type | solution.py:556
  140.1 1.2 bitcast_convert_fusion
Async XLA Ops:
  0.6 1.2 copy-start
  1.9 0.7 copy-start.1
  2.5 133.2 %copy-start.2 = (bf16[3,64,6144]{2,1,0:T(8,128)(2,1)S(1)}, bf16[3,64,6144]{2,1,0:T(8,128)(2,1)}, u32[]{:S(2)}) copy-start(bf16[3,64,6144]{2,1,0:T(8,128)(2,1)} %base_hbm.1) | copy-start | bytes 7077892
  2.5 133.2 %copy-start.3 = (f32[3,64,6144]{2,1,0:T(8,128)S(1)}, f32[3,64,6144]{2,1,0:T(8,128)}, u32[]{:S(2)}) copy-start(f32[3,64,6144]{2,1,0:T(8,128)} %param.8) | copy-start | bytes 14155780
